TPU v7x, 32 devices: a whole 2x2x4 slice. The times are simulated.
32 devices in a mesh: groups: 2 (over x), row: 8 (over z, y), col: 2 (over core).
Axes of the slice: x: 2, y: 2, z: 4, core: 2. Of those that a mesh axis runs over, the one named last changes fastest.
Arguments:
- sky_map: bfloat16 [512, 1024, 128], P(('groups', 'row'), 'col'), parts along dimension 0, may hold values from -6 to 6
- expand_weight: bfloat16 [128, 256], replicated, may hold values from -0.5 to 0.5
- expand_bias: float32 [256], replicated, may hold values from -3 to 3
- depth_weight: float32 [3, 3, 256], replicated, may hold values from -2 to 2
- depth_bias: float32 [256], replicated, may hold values from -3 to 3
- project_weight: bfloat16 [256, 128], replicated, may hold values from -0.375 to 0.375
- project_bias: float32 [128], replicated, may hold values from -3 to 3
- norm_gain: float32 [128], replicated, may hold values from 0.1 to 1.9
- norm_bias: float32 [128], replicated, may hold values from -3 to 3
- mixing_weight: bfloat16 [128, 384], replicated
- position_bias: float32 [4, 225], replicated, may hold values from -4 to 4
- output_weight: bfloat16 [128, 128], replicated, may hold values from -0.5 to 0.5
Outputs:
- block_out: bfloat16 [512, 1024, 128], P(('groups', 'row'), 'col'), parts along dimension 0
There are 2 independent parts, one for each index of `groups`. A program takes and returns all parts, laid end to end along the dimension named above; an argument that names none is the same for every part. Nothing has to cross between parts.
All inputs are finite; a program needn't handle non-finite values.
Results may differ from a plain program's by a relative error of at most 0.023.
Values may be sent and summed in bfloat16 or wider, within the bound.
A program may use at most 128 MiB of HBM per device.

v0:
```python
import functools
import math

import jax
import jax.numpy as jnp
from jax import lax
from jax.experimental import pallas as pl
from jax.experimental.pallas import tpu as pltpu
from jax.sharding import PartitionSpec as P

HEADS = 4
G = 8
EDGE = 16
LOG2E = math.log2(math.e)
MESH = pl.DeviceIdType.MESH
F32 = jnp.float32
BF16 = jnp.bfloat16


def gelu_tanh(values):
    half = 0.5 * values
    c0 = math.sqrt(2.0 / math.pi)
    return half * jnp.tanh(values * (c0 + (c0 * 0.044715) * (values * values))) + half


def kernel(
    sizes,
    sky,
    expand_weight,
    expand_bias,
    depth_weight,
    depth_bias,
    project_weight,
    project_bias,
    norm_gain,
    norm_bias,
    mixing_weight,
    table,
    head_mask,
    output_weight,
    out,
    halo_rows,
    halo_cols,
    expanded,
    side,
    t_left,
    t_mid,
    t_right,
    hidden,
    normed,
    received,
    group_in,
    group_out,
    attended,
    returned,
    halo_send,
    halo_recv,
    forward_send,
    forward_recv,
    back_send,
    back_recv,
):
    row_size, col_size = sizes
    rows, cols, channels = sky.shape
    chunks = rows // G
    across = G // col_size
    stride = cols // across
    width = stride // col_size
    tokens = G * G
    slots = G * col_size
    repeat = row_size // G

    face = lax.axis_index("groups")
    row = lax.axis_index("row")
    col = lax.axis_index("col")
    other = 1 - col
    my_p = row // repeat
    parity = row % repeat
    me = my_p * col_size + col
    has_up = row > 0
    has_down = row < row_size - 1

    def partner(j):
        slot = (me + 8 + ((j + 1) // 2) * (2 * (j % 2) - 1)) % slots
        p, c = slot // col_size, slot % col_size
        return slot, p, c, (face, p * repeat + parity, c)

    barrier = pltpu.get_barrier_semaphore()

    def greet(j, carry):
        pl.semaphore_signal(barrier, inc=1, device_id=partner(j)[3], device_id_type=MESH)
        return carry

    lax.fori_loop(0, slots - 1, greet, 0)
    pl.semaphore_wait(barrier, slots - 1)
    if repeat > 1:
        for there, near in ((has_up, row - 1), (has_down, row + 1)):

            @pl.when(there)
            def _():
                for c in (col, other):
                    pl.semaphore_signal(barrier, inc=1, device_id=(face, near, c), device_id_type=MESH)

        for there in (has_up, has_down):

            @pl.when(there)
            def _():
                pl.semaphore_wait(barrier, 2)

    edge_start = pl.multiple_of(other * (cols - EDGE), EDGE)
    edge = pl.ds(edge_start, EDGE)

    def remote(src, dst, i, j, device):
        return pltpu.make_async_remote_copy(
            src_ref=src,
            dst_ref=dst,
            send_sem=halo_send.at[i],
            recv_sem=halo_recv.at[j],
            device_id=device,
            device_id_type=MESH,
        )

    up_row = remote(sky.at[0], halo_rows.at[1], 0, 1, (face, row - 1, col))
    up_corner = remote(sky.at[0, edge], halo_cols.at[rows + 1], 1, 4, (face, row - 1, other))
    down_row = remote(sky.at[rows - 1], halo_rows.at[0], 2, 0, (face, row + 1, col))
    down_corner = remote(sky.at[rows - 1, edge], halo_cols.at[0], 3, 3, (face, row + 1, other))
    side_copy = remote(sky.at[:, edge], halo_cols.at[pl.ds(1, rows)], 4, 2, (face, row, other))

    @pl.when(has_up)
    def _():
        up_row.start()
        up_corner.start()

    @pl.when(has_down)
    def _():
        down_row.start()
        down_corner.start()

    side_copy.start()

    def expand(features):
        return gelu_tanh(
            jnp.dot(features, expand_weight[...], preferred_element_type=F32) + expand_bias[...]
        ).astype(BF16)

    def put_row(i, values):
        expanded[0, i] = values[:, :128]
        expanded[1, i] = values[:, 128:]

    def expand_row(i, carry):
        put_row(i + 1, expand(sky[i]))
        return carry

    lax.fori_loop(0, rows, expand_row, 0)

    side_copy.wait_recv()
    strip = expand(halo_cols[1 : rows + 1].reshape(rows * EDGE, channels)).astype(F32)
    side[0, 1 : rows + 1] = strip[:, :128].reshape(rows, EDGE, 128)
    side[1, 1 : rows + 1] = strip[:, 128:].reshape(rows, EDGE, 128)
    for there, slot, at, row_copy, corner_copy in (
        (has_up, 0, 0, down_row, down_corner),
        (has_down, 1, rows + 1, up_row, up_corner),
    ):

        @pl.when(there)
        def _():
            row_copy.wait_recv()
            corner_copy.wait_recv()
            put_row(at, expand(halo_rows[slot]))
            corner = expand(halo_cols[at]).astype(F32)
            side[0, at] = corner[:, :128]
            side[1, at] = corner[:, 128:]

        @pl.when(jnp.logical_not(there))
        def _():
            put_row(at, jnp.zeros((cols, 256), BF16))
            side[:, at] = jnp.zeros((2, EDGE, 128), F32)

    edge_at = other * 0 + col * (EDGE - 1)
    on_left = col.astype(F32)
    on_right = 1.0 - on_left
    tile = 128

    def conv_row(k, d):
        i = d * chunks + k
        for h in range(2):
            lanes = slice(h * 128, h * 128 + 128)
            taps = [[depth_weight[3 * a + b : 3 * a + b + 1, lanes] for b in range(3)] for a in range(3)]
            for j in range(0, cols, tile):
                cells = [expanded[h, i + a, j : j + tile, :].astype(F32) for a in range(3)]
                for b, buffer in ((0, t_left), (1, t_mid), (2, t_right)):
                    buffer[h, 8 + j : 8 + j + tile] = (
                        cells[0] * taps[0][b] + cells[1] * taps[1][b] + cells[2] * taps[2][b]
                    )
            beyond = [side[h, i + a, pl.ds(edge_at, 1), :] for a in range(3)]
            for b, buffer, at, on in ((0, t_left, 7, on_left), (2, t_right, 8 + cols, on_right)):
                buffer[h, at : at + 1] = on * (
                    beyond[0] * taps[0][b] + beyond[1] * taps[1][b] + beyond[2] * taps[2][b]
                )
            for j in range(0, cols, tile):
                total = (
                    t_left[h, 7 + j : 7 + j + tile]
                    + t_mid[h, 8 + j : 8 + j + tile]
                    + t_right[h, 9 + j : 9 + j + tile]
                    + depth_bias[:, lanes]
                )
                hidden[j : j + tile, lanes] = gelu_tanh(total).astype(BF16)
        for j in range(0, cols, tile):
            after = (
                sky[i, j : j + tile].astype(F32)
                + jnp.dot(hidden[j : j + tile], project_weight[...], preferred_element_type=F32)
                + project_bias[...]
            ).astype(BF16)
            out[i, j : j + tile] = after
            values = after.astype(F32)
            centred = values - jnp.mean(values, axis=-1, keepdims=True)
            variance = jnp.mean(centred * centred, axis=-1, keepdims=True)
            normed[k, d, j // stride, j % stride : j % stride + tile] = (
                centred * lax.rsqrt(variance + 1e-05) * norm_gain[...] + norm_bias[...]
            ).astype(BF16)

    def forward_copy(k, j):
        _, p, c, device = partner(j)
        return pltpu.make_async_remote_copy(
            src_ref=normed.at[k, p, :, pl.ds(pl.multiple_of(c * width, width), width)],
            dst_ref=received.at[k, me],
            send_sem=forward_send.at[k],
            recv_sem=forward_recv.at[k],
            device_id=device,
            device_id_type=MESH,
        )

    my_cols = pl.ds(pl.multiple_of(col * width, width), width)

    def back_copy(k, j):
        slot, _, _, device = partner(j)
        return pltpu.make_async_remote_copy(
            src_ref=attended.at[k, slot],
            dst_ref=returned.at[k, my_p, :, my_cols],
            send_sem=back_send.at[k],
            recv_sem=back_recv.at[k],
            device_id=device,
            device_id_type=MESH,
        )

    def conv_chunk(k, carry):
        def one(d, inner):
            conv_row(k, d)
            return inner

        lax.fori_loop(0, G, one, 0)

        def send(j, inner):
            forward_copy(k, j).start()
            return inner

        lax.fori_loop(0, slots - 1, send, 0)
        pltpu.make_async_copy(
            normed.at[k, my_p, :, my_cols], received.at[k, me], forward_recv.at[k]
        ).start()
        return carry

    lax.fori_loop(0, chunks, conv_chunk, 0)

    scale = LOG2E / math.sqrt(channels // HEADS)
    bundle = 8

    def attend_pair(first, second):
        keys, queries, values = [], [], []
        zero = jnp.zeros((tokens, channels), BF16)
        for projected in (first, second):
            key = projected[:, channels : 2 * channels]
            value = projected[:, 2 * channels :]
            keys.append(jnp.concatenate([key] * HEADS, axis=0) * head_mask[...])
            values.append(jnp.concatenate([value] * HEADS, axis=0) * head_mask[...])
        queries = jnp.concatenate(
            [
                jnp.concatenate([first[:, :channels], zero], axis=1),
                jnp.concatenate([zero, second[:, :channels]], axis=1),
            ],
            axis=0,
        )
        scores = lax.dot_general(
            jnp.concatenate(keys, axis=1),
            queries,
            (((1,), (1,)), ((), ())),
            preferred_element_type=F32,
        )
        scores = (scores * scale + table[...]).reshape(HEADS, tokens, 2 * tokens)
        powers = jnp.exp2(scores - jnp.max(scores, axis=1, keepdims=True))
        probs = powers * (1.0 / jnp.sum(powers, axis=1, keepdims=True))
        result = lax.dot_general(
            probs.astype(BF16).reshape(HEADS * tokens, 2 * tokens),
            jnp.concatenate(values, axis=1),
            (((0,), (0,)), ((), ())),
            preferred_element_type=F32,
        )
        return result[:tokens, :channels], result[tokens:, channels:]

    def attend_chunk(k, carry):
        pltpu.make_async_copy(received.at[k], received.at[k], forward_recv.at[k]).wait()

        def widen(s, inner):
            group_in[pl.ds(pl.multiple_of(s * across * width, across * width), across * width)] = (
                received[k, s].reshape(across * width, channels).astype(F32)
            )
            return inner

        lax.fori_loop(0, slots, widen, 0)

        def some_groups(b, inner):
            start = b * bundle
            features = jnp.concatenate(
                [group_in[pl.ds(start + n, tokens, stride=width), :] for n in range(bundle)], axis=0
            ).astype(BF16)
            projected = jnp.dot(features, mixing_weight[...], preferred_element_type=F32).astype(BF16)
            parts = [projected[n * tokens : (n + 1) * tokens] for n in range(bundle)]
            for n in range(0, bundle, 2):
                first, second = attend_pair(parts[n], parts[n + 1])
                group_out[pl.ds(start + n, tokens, stride=width), :] = first
                group_out[pl.ds(start + n + 1, tokens, stride=width), :] = second
            return inner

        lax.fori_loop(0, width // bundle, some_groups, 0)

        def narrow(s, inner):
            attended[k, s] = (
                group_out[pl.ds(pl.multiple_of(s * across * width, across * width), across * width)]
                .astype(BF16)
                .reshape(across, width, channels)
            )
            return inner

        lax.fori_loop(0, slots, narrow, 0)

        def send(j, inner):
            back_copy(k, j).start()
            return inner

        lax.fori_loop(0, slots - 1, send, 0)
        pltpu.make_async_copy(
            attended.at[k, me], returned.at[k, my_p, :, my_cols], back_recv.at[k]
        ).start()
        return carry

    lax.fori_loop(0, chunks, attend_chunk, 0)

    def finish_chunk(k, carry):
        pltpu.make_async_copy(returned.at[k], returned.at[k], back_recv.at[k]).wait()

        def one(d, inner):
            i = d * chunks + k
            out[i] = (
                out[i].astype(F32)
                + jnp.dot(
                    returned[k, d].reshape(cols, channels),
                    output_weight[...],
                    preferred_element_type=F32,
                )
            ).astype(BF16)
            return inner

        lax.fori_loop(0, G, one, 0)
        return carry

    lax.fori_loop(0, chunks, finish_chunk, 0)

    def drain(k, carry):
        sent = received.at[k, pl.ds(0, slots - 1)]
        pltpu.make_async_copy(sent, sent, forward_send.at[k]).wait()
        pltpu.make_async_copy(sent, sent, back_send.at[k]).wait()
        return carry

    lax.fori_loop(0, chunks, drain, 0)

    @pl.when(has_up)
    def _():
        up_row.wait_send()
        up_corner.wait_send()

    @pl.when(has_down)
    def _():
        down_row.wait_send()
        down_corner.wait_send()

    side_copy.wait_send()


def bias_table(position_bias):
    position = jnp.arange(G * G, dtype=jnp.int32)
    p, q = position // G, position % G
    offset = (p[None, :] - p[:, None] + G - 1) * (2 * G - 1) + (q[None, :] - q[:, None] + G - 1)
    entries = jnp.arange((2 * G - 1) ** 2, dtype=jnp.int32)
    one_hot = (offset[:, :, None] == entries[None, None, :]).astype(F32)
    table = jnp.einsum("ktn,hn->hkt", one_hot, position_bias, precision=lax.Precision.HIGHEST)
    table = table.reshape(-1, G * G) * LOG2E
    return jnp.concatenate([table, table], axis=1)


def body(
    sizes,
    sky_map,
    expand_weight,
    expand_bias,
    depth_weight,
    depth_bias,
    project_weight,
    project_bias,
    norm_gain,
    norm_bias,
    mixing_weight,
    position_bias,
    output_weight,
):
    rows, cols, channels = sky_map.shape
    wide = expand_weight.shape[1]
    col_size = sizes[1]
    chunks = rows // G
    across = G // col_size
    stride = cols // across
    width = stride // col_size
    slots = G * col_size
    tokens = G * G
    head_of = jnp.arange(HEADS * tokens, dtype=jnp.int32) // tokens
    lane_head = jnp.arange(channels, dtype=jnp.int32) // (channels // HEADS)
    head_mask = (head_of[:, None] == lane_head[None, :]).astype(BF16)
    vmem = pl.BlockSpec(memory_space=pltpu.VMEM)
    dma = pltpu.SemaphoreType.DMA
    return pl.pallas_call(
        functools.partial(kernel, sizes),
        out_shape=jax.ShapeDtypeStruct(sky_map.shape, BF16),
        in_specs=[vmem] * 13,
        out_specs=vmem,
        scratch_shapes=[
            pltpu.VMEM((2, cols, channels), BF16),
            pltpu.VMEM((rows + 2, EDGE, channels), BF16),
            pltpu.VMEM((2, rows + 2, cols, 128), BF16),
            pltpu.VMEM((2, rows + 2, EDGE, 128), F32),
            pltpu.VMEM((2, cols + 16, 128), F32),
            pltpu.VMEM((2, cols + 16, 128), F32),
            pltpu.VMEM((2, cols + 16, 128), F32),
            pltpu.VMEM((cols, wide), BF16),
            pltpu.VMEM((chunks, G, across, stride, channels), BF16),
            pltpu.VMEM((chunks, slots, across, width, channels), BF16),
            pltpu.VMEM((tokens * width, channels), F32),
            pltpu.VMEM((tokens * width, channels), F32),
            pltpu.VMEM((chunks, slots, across, width, channels), BF16),
            pltpu.VMEM((chunks, G, across, stride, channels), BF16),
            dma((5,)),
            dma((5,)),
            dma((chunks,)),
            dma((chunks,)),
            dma((chunks,)),
            dma((chunks,)),
        ],
        compiler_params=pltpu.CompilerParams(
            collective_id=0, has_side_effects=True, vmem_limit_bytes=58 * 1024 * 1024
        ),
    )(
        sky_map,
        expand_weight,
        expand_bias.reshape(1, wide),
        depth_weight.reshape(9, wide),
        depth_bias.reshape(1, wide),
        project_weight,
        project_bias.reshape(1, channels),
        norm_gain.reshape(1, channels),
        norm_bias.reshape(1, channels),
        mixing_weight,
        bias_table(position_bias),
        head_mask,
        output_weight,
    )


def solution(mesh):
    placed = (P(("groups", "row"), "col", None),) + (P(),) * 11
    sizes = (mesh.shape["row"], mesh.shape["col"])
    return jax.shard_map(
        functools.partial(body, sizes),
        mesh=mesh,
        in_specs=placed,
        out_specs=P(("groups", "row"), "col", None),
        check_vma=False,
    )
```

profile of v0, /device:TPU:13, one launch (start us, length us, event | category | flops | bytes accessed | tf_op | source)
XLA Modules:
  0.0 220.8 jit_solution(8937241633300505444)
XLA Ops:
  0.0 0.0 copy-start
  0.0 1.3 reshape.150.depth_weight
  1.3 0.1 add_add_fusion
  1.4 0.7 compare_convert_fusion.head_mask
  2.2 0.0 copy-done
  2.2 2.8 %fusion.3 = f32[4,64,64]{2,0,1:T(4,128)S(1)} fusion(s32[64,64]{1,0:T(8,128)S(1)} %add_add_fusion, f32[4,225]{1,0:T(4,128)S(1)} %copy-done), kind=kOutput, calls=%fused_computation.4 | convolution fusion | flops 45174784 | bytes 85520 | tf_op jit(solution)/shard_map/ktn,hn->hkt/dot_general | solution.py:395
  5.0 0.8 pad_maximum_fusion.table
  5.8 210.4 %shard_map.118 = bf16[32,512,128]{2,1,0:T(8,128)(2,1)} custom-call(bf16[32,512,128]{2,1,0:T(8,128)(2,1)} %sky.1, bf16[128,256]{1,0:T(8,128)(2,1)} %expand_weight.1, f32[1,256]{1,0:T(1,128)} %bitcast.12, f32[9,256]{1,0:T(8,128)} %reshape.150.depth_weight, f32[1,256]{1,0:T(1,128)} %bitcast.13, bf16[256,128]{1,0:T(8,128)(2,1)} %project_weight.1, ...), custom_call_target="tpu_custom_call" | custom-call | tf_op jit(solution)/shard_map/pallas_call | solution.py:429
  216.1 4.7 %copy.15 = bf16[32,512,128]{2,1,0:T(8,128)(2,1)} copy(bf16[32,512,128]{2,1,0:T(8,128)(2,1)} %shard_map.118) | data formatting | bytes 8388608
  (4 shorter events, 0.0 us)
Async XLA Ops:
  0.0 2.2 copy-start
where the time goes:
time: 222 us; the launch traced here: 221 us
  Pallas kernels  210 us (95%)
  local copies, waits for them, and re-layouts  6 us (3%)
  matrix products  2.8 us (1%)
    pallas_call x1, Pallas kernels, body(): pl.pallas_call(functools.partial(kernel, sizes), out_shape=jax.ShapeDtype...  210 us
    unnamed x3, local copies, waits for them, and re-layouts  4.66 us

commit v1 on v0

--- a/solution.py
+++ b/solution.py
@@ -21,6 +21,29 @@
     half = 0.5 * values
     c0 = math.sqrt(2.0 / math.pi)
     return half * jnp.tanh(values * (c0 + (c0 * 0.044715) * (values * values))) + half
+
+
+def make_tables(position_bias, shifted, table, head_mask):
+    tokens = G * G
+    side = 2 * G - 1
+    reach = (G - 1) * side + G
+    shifted[...] = jnp.zeros(shifted.shape, F32)
+    for u in range(tokens):
+        offset = (G - 1 - u // G) * side + (G - 1 - u % G)
+        for h in range(HEADS):
+            shifted[h * tokens + u : h * tokens + u + 1, :reach] = position_bias[
+                h : h + 1, offset : offset + reach
+            ]
+    lane = lax.broadcasted_iota(jnp.int32, (128, 2 * tokens), 1) % tokens
+    entry = lax.broadcasted_iota(jnp.int32, (128, 2 * tokens), 0)
+    pick = (entry == (lane // G) * side + lane % G).astype(F32)
+    table[...] = LOG2E * jnp.dot(
+        shifted[...], pick, precision=lax.Precision.HIGHEST, preferred_element_type=F32
+    )
+    channels = head_mask.shape[1]
+    of_row = lax.broadcasted_iota(jnp.int32, head_mask.shape, 0) // tokens
+    of_lane = lax.broadcasted_iota(jnp.int32, head_mask.shape, 1) // (channels // HEADS)
+    head_mask[...] = (of_row == of_lane).astype(F32).astype(BF16)
 
 
 def kernel(
@@ -35,8 +58,7 @@
     norm_gain,
     norm_bias,
     mixing_weight,
-    table,
-    head_mask,
+    position_bias,
     output_weight,
     out,
     halo_rows,
@@ -55,6 +77,9 @@
     returned,
     halo_send,
     halo_recv,
+    shifted,
+    table,
+    head_mask,
     forward_send,
     forward_recv,
     back_send,
@@ -147,11 +172,25 @@
         expanded[0, i] = values[:, :128]
         expanded[1, i] = values[:, 128:]
 
-    def expand_row(i, carry):
+    def expand_row(i):
         put_row(i + 1, expand(sky[i]))
-        return carry
-
-    lax.fori_loop(0, rows, expand_row, 0)
+
+    half = G // 2
+    far = (my_p // half + 1) % 2 * half
+
+    def target(j):
+        return (far + (my_p + j) % half + (j // half) * half) % G
+
+    def expand_first(j):
+        i = target(j) * chunks
+        expand_row(i)
+        expand_row(i + 1)
+
+        @pl.when(i > 0)
+        def _():
+            expand_row(i - 1)
+
+    expand_first(0)
 
     side_copy.wait_recv()
     strip = expand(halo_cols[1 : rows + 1].reshape(rows * EDGE, channels)).astype(F32)
@@ -185,7 +224,7 @@
         i = d * chunks + k
         for h in range(2):
             lanes = slice(h * 128, h * 128 + 128)
-            taps = [[depth_weight[3 * a + b : 3 * a + b + 1, lanes] for b in range(3)] for a in range(3)]
+            taps = [[depth_weight[a, b : b + 1, lanes] for b in range(3)] for a in range(3)]
             for j in range(0, cols, tile):
                 cells = [expanded[h, i + a, j : j + tile, :].astype(F32) for a in range(3)]
                 for b, buffer in ((0, t_left), (1, t_mid), (2, t_right)):
@@ -219,14 +258,13 @@
                 centred * lax.rsqrt(variance + 1e-05) * norm_gain[...] + norm_bias[...]
             ).astype(BF16)
 
-    def forward_copy(k, j):
-        _, p, c, device = partner(j)
+    def forward_copy(k, p, c):
         return pltpu.make_async_remote_copy(
-            src_ref=normed.at[k, p, :, pl.ds(pl.multiple_of(c * width, width), width)],
+            src_ref=normed.at[k, p, :, pl.ds(c * width, width)],
             dst_ref=received.at[k, me],
             send_sem=forward_send.at[k],
             recv_sem=forward_recv.at[k],
-            device_id=device,
+            device_id=(face, p * repeat + parity, c),
             device_id_type=MESH,
         )
 
@@ -243,26 +281,42 @@
             device_id_type=MESH,
         )
 
-    def conv_chunk(k, carry):
-        def one(d, inner):
-            conv_row(k, d)
-            return inner
-
-        lax.fori_loop(0, G, one, 0)
-
-        def send(j, inner):
-            forward_copy(k, j).start()
-            return inner
-
-        lax.fori_loop(0, slots - 1, send, 0)
-        pltpu.make_async_copy(
-            normed.at[k, my_p, :, my_cols], received.at[k, me], forward_recv.at[k]
-        ).start()
+    def conv_step(s, carry):
+        k, j = s // G, s % G
+        d = target(j)
+
+        @pl.when((k > 0) & (k < chunks - 2))
+        def _():
+            expand_row(d * chunks + k + 1)
+
+        conv_row(k, d)
+        for c in range(col_size):
+            mine = (d == my_p) & (c == col)
+
+            @pl.when(jnp.logical_not(mine))
+            def _():
+                forward_copy(k, d, c).start()
+
+            @pl.when(mine)
+            def _():
+                pltpu.make_async_copy(
+                    normed.at[k, my_p, :, my_cols], received.at[k, me], forward_recv.at[k]
+                ).start()
+
+        @pl.when((k == 0) & (j < G - 1))
+        def _():
+            expand_first(j + 1)
+
+        @pl.when((k == 0) & (j == G - 1))
+        def _():
+            expand_row(rows - 1)
+
         return carry
 
-    lax.fori_loop(0, chunks, conv_chunk, 0)
+    lax.fori_loop(0, chunks * G, conv_step, 0)
 
     scale = LOG2E / math.sqrt(channels // HEADS)
+    make_tables(position_bias, shifted, table, head_mask)
     bundle = 8
 
     def attend_pair(first, second):
@@ -386,17 +440,6 @@
     side_copy.wait_send()
 
 
-def bias_table(position_bias):
-    position = jnp.arange(G * G, dtype=jnp.int32)
-    p, q = position // G, position % G
-    offset = (p[None, :] - p[:, None] + G - 1) * (2 * G - 1) + (q[None, :] - q[:, None] + G - 1)
-    entries = jnp.arange((2 * G - 1) ** 2, dtype=jnp.int32)
-    one_hot = (offset[:, :, None] == entries[None, None, :]).astype(F32)
-    table = jnp.einsum("ktn,hn->hkt", one_hot, position_bias, precision=lax.Precision.HIGHEST)
-    table = table.reshape(-1, G * G) * LOG2E
-    return jnp.concatenate([table, table], axis=1)
-
-
 def body(
     sizes,
     sky_map,
@@ -421,15 +464,12 @@
     width = stride // col_size
     slots = G * col_size
     tokens = G * G
-    head_of = jnp.arange(HEADS * tokens, dtype=jnp.int32) // tokens
-    lane_head = jnp.arange(channels, dtype=jnp.int32) // (channels // HEADS)
-    head_mask = (head_of[:, None] == lane_head[None, :]).astype(BF16)
     vmem = pl.BlockSpec(memory_space=pltpu.VMEM)
     dma = pltpu.SemaphoreType.DMA
     return pl.pallas_call(
         functools.partial(kernel, sizes),
         out_shape=jax.ShapeDtypeStruct(sky_map.shape, BF16),
-        in_specs=[vmem] * 13,
+        in_specs=[vmem] * 12,
         out_specs=vmem,
         scratch_shapes=[
             pltpu.VMEM((2, cols, channels), BF16),
@@ -448,6 +488,9 @@
             pltpu.VMEM((chunks, G, across, stride, channels), BF16),
             dma((5,)),
             dma((5,)),
+            pltpu.VMEM((HEADS * tokens, 128), F32),
+            pltpu.VMEM((HEADS * tokens, 2 * tokens), F32),
+            pltpu.VMEM((HEADS * tokens, channels), BF16),
             dma((chunks,)),
             dma((chunks,)),
             dma((chunks,)),
@@ -460,15 +503,14 @@
         sky_map,
         expand_weight,
         expand_bias.reshape(1, wide),
-        depth_weight.reshape(9, wide),
+        depth_weight,
         depth_bias.reshape(1, wide),
         project_weight,
         project_bias.reshape(1, channels),
         norm_gain.reshape(1, channels),
         norm_bias.reshape(1, channels),
         mixing_weight,
-        bias_table(position_bias),
-        head_mask,
+        position_bias,
         output_weight,
     )
 

time: 222 us -> 206 us (0.928)
  Pallas kernels: 210 us -> 202 us
  matrix products: 2.8 us -> 0 us
    pallas_call x1, Pallas kernels: 210 us -> 202 us  [body(): pl.pallas_call(functools.partial(kernel, sizes), out_shape=jax.ShapeDtype...]
    dot_general x1 -> x0, matrix products: 2.8 us -> none  [bias_table(): jnp.einsum('ktn,hn->hkt', one_hot, position_bias, precision=lax.Precision...]
    unnamed x3 -> x1, local copies, waits for them, and re-layouts: 4.66 us -> 4.65 us
where the time goes in v1:
time: 206 us
  Pallas kernels  202 us (98%)
  local copies, waits for them, and re-layouts  4.65 us (2%)
    pallas_call x1, Pallas kernels, body(): pl.pallas_call(functools.partial(kernel, sizes), out_shape=jax.ShapeDtype...  202 us
    unnamed x1, local copies, waits for them, and re-layouts  4.65 us

profile of v1, /device:TPU:13, one launch (start us, length us, event | category | flops | bytes accessed | tf_op | source)
XLA Modules:
  0.0 206.3 jit_solution(13952720820402327141)
XLA Ops:
  0.0 201.7 %shard_map.118 = bf16[32,512,128]{2,1,0:T(8,128)(2,1)} custom-call(bf16[32,512,128]{2,1,0:T(8,128)(2,1)} %sky.1, bf16[128,256]{1,0:T(8,128)(2,1)} %expand_weight.1, f32[1,256]{1,0:T(1,128)} %bitcast.5, f32[3,3,256]{2,1,0:T(4,128)} %depth_weight.1, f32[1,256]{1,0:T(1,128)} %bitcast.6, bf16[256,128]{1,0:T(8,128)(2,1)} %project_weight.1, f32[1,128]{1,0:T(1,128)} %bitcast.7, ...), custom_call_target="tpu_custom_call" | custom-call | tf_op jit(solution)/shard_map/pallas_call | solution.py:469
  201.7 4.7 %copy.14 = bf16[32,512,128]{2,1,0:T(8,128)(2,1)} copy(bf16[32,512,128]{2,1,0:T(8,128)(2,1)} %shard_map.118) | data formatting | bytes 8388608

commit v2 on v1

--- a/solution.py
+++ b/solution.py
@@ -48,7 +48,7 @@
 
 def kernel(
     sizes,
-    sky,
+    sky_map,
     expand_weight,
     expand_bias,
     depth_weight,
@@ -60,6 +60,8 @@
     mixing_weight,
     position_bias,
     output_weight,
+    block_out,
+    sky,
     out,
     halo_rows,
     halo_cols,
@@ -84,6 +86,8 @@
     forward_recv,
     back_send,
     back_recv,
+    load_sem,
+    store_sem,
 ):
     row_size, col_size = sizes
     rows, cols, channels = sky.shape
@@ -110,6 +114,15 @@
         p, c = slot // col_size, slot % col_size
         return slot, p, c, (face, p * repeat + parity, c)
 
+    part = rows // load_sem.shape[0]
+    loads = [
+        pltpu.make_async_copy(
+            sky_map.at[pl.ds(n * part, part)], sky.at[pl.ds(n * part, part)], load_sem.at[n]
+        )
+        for n in range(load_sem.shape[0])
+    ]
+    for load in loads:
+        load.start()
     barrier = pltpu.get_barrier_semaphore()
 
     def greet(j, carry):
@@ -145,11 +158,11 @@
             device_id_type=MESH,
         )
 
-    up_row = remote(sky.at[0], halo_rows.at[1], 0, 1, (face, row - 1, col))
-    up_corner = remote(sky.at[0, edge], halo_cols.at[rows + 1], 1, 4, (face, row - 1, other))
-    down_row = remote(sky.at[rows - 1], halo_rows.at[0], 2, 0, (face, row + 1, col))
-    down_corner = remote(sky.at[rows - 1, edge], halo_cols.at[0], 3, 3, (face, row + 1, other))
-    side_copy = remote(sky.at[:, edge], halo_cols.at[pl.ds(1, rows)], 4, 2, (face, row, other))
+    up_row = remote(sky_map.at[0], halo_rows.at[1], 0, 1, (face, row - 1, col))
+    up_corner = remote(sky_map.at[0, edge], halo_cols.at[rows + 1], 1, 4, (face, row - 1, other))
+    down_row = remote(sky_map.at[rows - 1], halo_rows.at[0], 2, 0, (face, row + 1, col))
+    down_corner = remote(sky_map.at[rows - 1, edge], halo_cols.at[0], 3, 3, (face, row + 1, other))
+    side_copy = remote(sky_map.at[:, edge], halo_cols.at[pl.ds(1, rows)], 4, 2, (face, row, other))
 
     @pl.when(has_up)
     def _():
@@ -190,6 +203,8 @@
         def _():
             expand_row(i - 1)
 
+    for load in loads:
+        load.wait()
     expand_first(0)
 
     side_copy.wait_recv()
@@ -412,6 +427,7 @@
                     preferred_element_type=F32,
                 )
             ).astype(BF16)
+            pltpu.make_async_copy(out.at[i], block_out.at[i], store_sem.at[k]).start()
             return inner
 
         lax.fori_loop(0, G, one, 0)
@@ -423,6 +439,8 @@
         sent = received.at[k, pl.ds(0, slots - 1)]
         pltpu.make_async_copy(sent, sent, forward_send.at[k]).wait()
         pltpu.make_async_copy(sent, sent, back_send.at[k]).wait()
+        stored = out.at[pl.ds(0, G)]
+        pltpu.make_async_copy(stored, stored, store_sem.at[k]).wait()
         return carry
 
     lax.fori_loop(0, chunks, drain, 0)
@@ -465,13 +483,16 @@
     slots = G * col_size
     tokens = G * G
     vmem = pl.BlockSpec(memory_space=pltpu.VMEM)
+    anywhere = pl.BlockSpec(memory_space=pl.ANY)
     dma = pltpu.SemaphoreType.DMA
     return pl.pallas_call(
         functools.partial(kernel, sizes),
         out_shape=jax.ShapeDtypeStruct(sky_map.shape, BF16),
-        in_specs=[vmem] * 12,
-        out_specs=vmem,
+        in_specs=[anywhere] + [vmem] * 11,
+        out_specs=anywhere,
         scratch_shapes=[
+            pltpu.VMEM(sky_map.shape, BF16),
+            pltpu.VMEM(sky_map.shape, BF16),
             pltpu.VMEM((2, cols, channels), BF16),
             pltpu.VMEM((rows + 2, EDGE, channels), BF16),
             pltpu.VMEM((2, rows + 2, cols, 128), BF16),
@@ -495,6 +516,8 @@
             dma((chunks,)),
             dma((chunks,)),
             dma((chunks,)),
+            dma((4,)),
+            dma((chunks,)),
         ],
         compiler_params=pltpu.CompilerParams(
             collective_id=0, has_side_effects=True, vmem_limit_bytes=58 * 1024 * 1024

time: 206 us -> 204 us (level)
    pallas_call x1, Pallas kernels: 202 us -> 200 us  [body(): pl.pallas_call(functools.partial(kernel, sizes), out_shape=jax.ShapeDtype...]
where the time goes in v2:
time: 204 us
  Pallas kernels  200 us (98%)
  local copies, waits for them, and re-layouts  4.65 us (2%)
    pallas_call x1, Pallas kernels, body(): pl.pallas_call(functools.partial(kernel, sizes), out_shape=jax.ShapeDtype...  200 us
    unnamed x1, local copies, waits for them, and re-layouts  4.65 us

profile of v2, /device:TPU:13, one launch (start us, length us, event | category | flops | bytes accessed | tf_op | source)
XLA Modules:
  0.0 204.2 jit_solution(13394404734640109700)
XLA Ops:
  0.0 199.6 %shard_map.118 = bf16[32,512,128]{2,1,0:T(8,128)(2,1)} custom-call(bf16[32,512,128]{2,1,0:T(8,128)(2,1)} %sky_map.1, bf16[128,256]{1,0:T(8,128)(2,1)} %expand_weight.1, f32[1,256]{1,0:T(1,128)} %bitcast.5, f32[3,3,256]{2,1,0:T(4,128)} %depth_weight.1, f32[1,256]{1,0:T(1,128)} %bitcast.6, bf16[256,128]{1,0:T(8,128)(2,1)} %project_weight.1, f32[1,128]{1,0:T(1,128)} %bitcast.7, ...), custom_call_target="tpu_custom_call" | custom-call | tf_op jit(solution)/shard_map/pallas_call | solution.py:488
  199.6 4.7 %copy.14 = bf16[32,512,128]{2,1,0:T(8,128)(2,1)} copy(bf16[32,512,128]{2,1,0:T(8,128)(2,1)} %shard_map.118) | data formatting | bytes 8388608

commit v3 on v2

--- a/solution.py
+++ b/solution.py
@@ -285,8 +285,9 @@
 
     my_cols = pl.ds(pl.multiple_of(col * width, width), width)
 
-    def back_copy(k, j):
-        slot, _, _, device = partner(j)
+    def back_copy(k, p, c):
+        slot = p * col_size + c
+        device = (face, p * repeat + parity, c)
         return pltpu.make_async_remote_copy(
             src_ref=attended.at[k, slot],
             dst_ref=returned.at[k, my_p, :, my_cols],
@@ -403,10 +404,16 @@
         lax.fori_loop(0, slots, narrow, 0)
 
         def send(j, inner):
-            back_copy(k, j).start()
+            p = target(j)
+            for c in range(col_size):
+
+                @pl.when(jnp.logical_not((p == my_p) & (c == col)))
+                def _():
+                    back_copy(k, p, c).start()
+
             return inner
 
-        lax.fori_loop(0, slots - 1, send, 0)
+        lax.fori_loop(0, G, send, 0)
         pltpu.make_async_copy(
             attended.at[k, me], returned.at[k, my_p, :, my_cols], back_recv.at[k]
         ).start()

time: 204 us -> 205 us (level)
  no operation moved by 1% of the time
where the time goes in v3:
time: 205 us
  Pallas kernels  200 us (98%)
  local copies, waits for them, and re-layouts  4.65 us (2%)
    pallas_call x1, Pallas kernels, body(): pl.pallas_call(functools.partial(kernel, sizes), out_shape=jax.ShapeDtype...  200 us
    unnamed x1, local copies, waits for them, and re-layouts  4.65 us

profile of v3, /device:TPU:13, one launch (start us, length us, event | category | flops | bytes accessed | tf_op | source)
XLA Modules:
  0.0 204.9 jit_solution(3039344661863212569)
XLA Ops:
  0.0 200.2 %shard_map.118 = bf16[32,512,128]{2,1,0:T(8,128)(2,1)} custom-call(bf16[32,512,128]{2,1,0:T(8,128)(2,1)} %sky_map.1, bf16[128,256]{1,0:T(8,128)(2,1)} %expand_weight.1, f32[1,256]{1,0:T(1,128)} %bitcast.5, f32[3,3,256]{2,1,0:T(4,128)} %depth_weight.1, f32[1,256]{1,0:T(1,128)} %bitcast.6, bf16[256,128]{1,0:T(8,128)(2,1)} %project_weight.1, f32[1,128]{1,0:T(1,128)} %bitcast.7, ...), custom_call_target="tpu_custom_call" | custom-call | tf_op jit(solution)/shard_map/pallas_call | solution.py:495
  200.2 4.7 %copy.14 = bf16[32,512,128]{2,1,0:T(8,128)(2,1)} copy(bf16[32,512,128]{2,1,0:T(8,128)(2,1)} %shard_map.118) | data formatting | bytes 8388608
